TPU v7x, 32 devices: a whole 2x2x4 slice. The times are simulated.
32 devices in a mesh: groups: 2 (over x), expert: 16 (over z, y, core).
Axes of the slice: x: 2, y: 2, z: 4, core: 2. Of those that a mesh axis runs over, the one named last changes fastest.
Arguments:
- tokens: bfloat16 [4096, 2048], P(('groups', 'expert')), parts along dimension 0, may hold values from -12 to 12
- out_grad: bfloat16 [4096, 2048], P(('groups', 'expert')), parts along dimension 0, may hold values from -6 to 6
- cluster_ids: int32 [4096], P(('groups', 'expert')), parts along dimension 0, may hold values from 0 to 31, as said below
- routes: int32 [1024, 8], P(('groups', 'expert')), parts along dimension 0, may hold values from 0 to 15, all different within a row; in each aligned block of 32 rows (0 to 31, 32 to 63, ...) at most 32 rows name the same one
- route_weights: float32 [1024, 8], P(('groups', 'expert')), parts along dimension 0, may hold values from 0.05 to 0.5
- gate_weight: bfloat16 [16, 2048, 768], P('expert'), may hold values from -0.125 to 0.125
- up_weight: bfloat16 [16, 2048, 768], P('expert'), may hold values from -0.125 to 0.125
- down_weight: bfloat16 [16, 768, 2048], P('expert'), may hold values from -0.21875 to 0.21875
Outputs:
- layer_out: float32 [4096, 2048], P(('groups', 'expert')), parts along dimension 0
- token_grad: float32 [4096, 2048], P(('groups', 'expert')), parts along dimension 0
There are 2 independent parts, one for each index of `groups`. A program takes and returns all parts, laid end to end along the dimension named above; an argument that names none is the same for every part. Nothing has to cross between parts.
Inputs may be any that keep to these rules, and one draw needn't show every extreme that they name: `cluster_ids`: within each block of 128 tokens every one of the 32 cluster numbers occurs at least once. `routes`: each row names 8 different experts. Among the 32 rows of one index of expert no expert is named more than 32 times, and in some such blocks one expert is named exactly 32 times.
All inputs are finite; a program needn't handle non-finite values.
Results may differ from a plain program's by a relative error of at most 0.0027.
Values may be sent and summed in bfloat16 or wider, within the bound.
A program may use at most 64 MiB of HBM per device.

v0:
```python
import jax
import jax.numpy as jnp
from jax import lax
from jax.sharding import PartitionSpec as P


def expert_forward(inputs, gate_mat, up_mat, down_mat):
    gate_act = jnp.dot(inputs, gate_mat, preferred_element_type=jnp.float32)
    up_act = jnp.dot(inputs, up_mat, preferred_element_type=jnp.float32)
    sigmoid_gate = jax.nn.sigmoid(gate_act)
    hidden = (gate_act * sigmoid_gate * up_act).astype(jnp.bfloat16)
    output = jnp.dot(hidden, down_mat, preferred_element_type=jnp.float32).astype(jnp.bfloat16)
    return (output, gate_act, up_act)


def expert_backward(incoming, gate_act, up_act, gate_mat, up_mat, down_mat):
    against = (((1,), (1,)), ((), ()))
    hidden_grad = lax.dot_general(incoming, down_mat, against, preferred_element_type=jnp.float32)
    sigmoid_gate = jax.nn.sigmoid(gate_act)
    gate_grad = (
        hidden_grad * up_act * sigmoid_gate * (1.0 + gate_act * (1.0 - sigmoid_gate))
    ).astype(jnp.bfloat16)
    up_grad = (hidden_grad * gate_act * sigmoid_gate).astype(jnp.bfloat16)
    summed = lax.dot_general(gate_grad, gate_mat, against, preferred_element_type=jnp.float32)
    summed = summed + lax.dot_general(up_grad, up_mat, against, preferred_element_type=jnp.float32)
    return summed.astype(jnp.bfloat16)


def per_device(
    tokens, out_grad, cluster_ids, routes, route_weights, gate_weight, up_weight, down_weight
):
    model_width = tokens.shape[1]
    cent_rows = routes.shape[0]
    fanout = routes.shape[1]
    experts = lax.axis_size("expert")
    capacity = min(cent_rows, 2 * cent_rows * fanout // experts)
    member = (cluster_ids[:, None] == jnp.arange(cent_rows, dtype=jnp.int32)[None, :]).astype(
        jnp.bfloat16
    )
    counts = jnp.sum(member.astype(jnp.float32), axis=0)
    contract = (((0,), (0,)), ((), ()))
    centroid = (
        lax.dot_general(member, tokens, contract, preferred_element_type=jnp.float32)
        / counts[:, None]
    )
    grad_sum = lax.dot_general(member, out_grad, contract, preferred_element_type=jnp.float32)
    pair_ids = routes.reshape(-1)
    matches = (pair_ids[:, None] == jnp.arange(experts, dtype=jnp.int32)[None, :]).astype(jnp.int32)
    earlier = jnp.cumsum(matches, axis=0) - matches
    position = jnp.sum(earlier * matches, axis=1)
    slot_of = (pair_ids * capacity + position).reshape(cent_rows, fanout)
    slot_range = jnp.arange(experts * capacity, dtype=jnp.int32)
    placing = jnp.any(slot_of[None, :, :] == slot_range[:, None, None], axis=2).astype(jnp.bfloat16)
    send_cent = jnp.dot(placing, centroid.astype(jnp.bfloat16), preferred_element_type=jnp.float32)
    send_cent = send_cent.astype(jnp.bfloat16).reshape(experts, capacity, model_width)
    send_grad = jnp.dot(placing, grad_sum.astype(jnp.bfloat16), preferred_element_type=jnp.float32)
    send_grad = send_grad.astype(jnp.bfloat16).reshape(experts, capacity, model_width)
    gate_mat = gate_weight[0]
    up_mat = up_weight[0]
    down_mat = down_weight[0]
    arrived = lax.all_to_all(send_cent, "expert", split_axis=0, concat_axis=0, tiled=True)
    output, gate_act, up_act = expert_forward(
        arrived.reshape(-1, model_width), gate_mat, up_mat, down_mat
    )
    results = lax.all_to_all(
        output.reshape(experts, capacity, model_width),
        "expert",
        split_axis=0,
        concat_axis=0,
        tiled=True,
    )
    arrived_grad = lax.all_to_all(send_grad, "expert", split_axis=0, concat_axis=0, tiled=True)
    input_grad = expert_backward(
        arrived_grad.reshape(-1, model_width), gate_act, up_act, gate_mat, up_mat, down_mat
    )
    results_grad = lax.all_to_all(
        input_grad.reshape(experts, capacity, model_width),
        "expert",
        split_axis=0,
        concat_axis=0,
        tiled=True,
    )
    returned = results.reshape(-1, model_width)[slot_of]
    returned_grad = results_grad.reshape(-1, model_width)[slot_of]
    combined = jnp.sum(route_weights[:, :, None] * returned.astype(jnp.float32), axis=1)
    centroid_grad = (
        jnp.sum(route_weights[:, :, None] * returned_grad.astype(jnp.float32), axis=1) - grad_sum
    )
    layer_out = tokens.astype(jnp.float32) + jnp.take(combined - centroid, cluster_ids, axis=0)
    token_grad = out_grad.astype(jnp.float32) + jnp.take(
        centroid_grad / counts[:, None], cluster_ids, axis=0
    )
    return (layer_out, token_grad)


def solution(mesh):
    placed = (
        P(("groups", "expert"), None),
        P(("groups", "expert"), None),
        P(("groups", "expert")),
        P(("groups", "expert"), None),
        P(("groups", "expert"), None),
        P("expert", None, None),
        P("expert", None, None),
        P("expert", None, None),
    )
    return jax.shard_map(
        per_device,
        mesh=mesh,
        in_specs=placed,
        out_specs=(P(("groups", "expert"), None), P(("groups", "expert"), None)),
        check_vma=False,
    )
```

profile of v0, /device:TPU:13, one launch (start us, length us, event | category | flops | bytes accessed | tf_op | source)
XLA Modules:
  0.0 248.2 jit_solution(3509352852602041339)
XLA Ops:
  0.6 0.0 copy-start
  0.6 0.9 copy.18
  1.6 0.1 eq.55
  1.6 0.1 eq.51
  1.8 0.6 reduce-window.6
  2.3 0.2 slice_reduce_fusion
  2.6 0.1 fusion.27
  2.7 0.1 reduce_sum.39
  2.8 0.2 fusion.22
  3.0 0.8 convert_reduce_fusion
  3.8 1.3 convolution_divide_fusion
  5.0 0.0 copy-start.3
  5.1 0.7 copy-done.3
  5.7 2.1 convolution_convert_fusion.1
  7.8 6.7 %all-to-all-start = ((bf16[16,32,2048]{2,1,0:T(8,128)(2,1)}), bf16[16,32,2048]{2,1,0:T(8,128)(2,1)}, u32[]{:S(2)}, u32[]{:S(2)}) async-start(bf16[16,32,2048]{2,1,0:T(8,128)(2,1)} %bitcast.60), calls=%async_computation | async-start | bytes 4194304 | tf_op jit(solution)/shard_map/all_to_all | solution.py:61
  14.5 0.0 copy-done.6
  14.5 1.2 fusion.28
  15.8 0.0 copy-start.1
  15.8 0.7 copy-done.1
  16.5 2.1 convolution_convert_fusion
  18.5 43.5 %all-to-all-done = bf16[16,32,2048]{2,1,0:T(8,128)(2,1)} async-done(((bf16[16,32,2048]{2,1,0:T(8,128)(2,1)}), bf16[16,32,2048]{2,1,0:T(8,128)(2,1)}, u32[]{:S(2)}, u32[]{:S(2)}) %all-to-all-start) | async-done | bytes 2097184 | tf_op jit(solution)/shard_map/all_to_all | solution.py:61
  62.0 4.9 %all-to-all-start.2 = ((bf16[16,32,2048]{2,1,0:T(8,128)(2,1)}), bf16[16,32,2048]{2,1,0:T(8,128)(2,1)}, u32[]{:S(2)}, u32[]{:S(2)}) async-start(bf16[16,32,2048]{2,1,0:T(8,128)(2,1)} %bitcast.59), calls=%async_computation.2 | async-start | bytes 4194304 | tf_op jit(solution)/shard_map/all_to_all | solution.py:72
  67.0 5.5 %fusion.10 = f32[512,768]{1,0:T(8,128)} fusion(bf16[512,2048]{1,0:T(8,128)(2,1)} %bitcast.2, bf16[1,2048,768]{2,1,0:T(8,128)(2,1)} %param.15), kind=kOutput, calls=%fused_computation.15 | convolution fusion | flops 1610612736 | bytes 6815744 | tf_op jit(solution)/shard_map/dot_general | solution.py:8
  72.4 0.0 copy-done
  72.4 4.6 %fusion.6 = f32[512,768]{1,0:T(8,128)} fusion(bf16[512,2048]{1,0:T(8,128)(2,1)} %bitcast.2, bf16[1,2048,768]{2,1,0:T(8,128)(2,1)S(1)} %copy-done), kind=kOutput, calls=%fused_computation.11 | convolution fusion | flops 1610612736 | bytes 6815744 | tf_op jit(solution)/shard_map/dot_general | solution.py:9
  77.0 37.5 %all-to-all-done.2 = bf16[16,32,2048]{2,1,0:T(8,128)(2,1)} async-done(((bf16[16,32,2048]{2,1,0:T(8,128)(2,1)}), bf16[16,32,2048]{2,1,0:T(8,128)(2,1)}, u32[]{:S(2)}, u32[]{:S(2)}) %all-to-all-start.2) | async-done | bytes 2097184 | tf_op jit(solution)/shard_map/all_to_all | solution.py:72
  114.5 4.5 %fusion = f32[512,768]{1,0:T(8,128)S(1)} fusion(bf16[512,2048]{1,0:T(8,128)(2,1)} %bitcast.10, bf16[1,768,2048]{2,1,0:T(8,128)(2,1)} %param.17), kind=kOutput, calls=%fused_computation.5 | convolution fusion | flops 1610612736 | bytes 6815744 | tf_op jit(solution)/shard_map/dot_general | solution.py:18
  119.0 0.0 copy-start.7
  119.0 1.9 fusion.4
  120.8 0.0 copy-done.7
  120.9 0.5 copy-done.9
  121.3 3.6 %add_convert_fusion = bf16[512,2048]{1,0:T(8,128)(2,1)} fusion(f32[512,2048]{1,0:T(8,128)S(1)} %fusion.4, bf16[1,2048,768]{2,1,0:T(8,128)(2,1)S(1)} %copy-done.7, f32[512,768]{1,0:T(8,128)S(1)} %copy-done.8, f32[512,768]{1,0:T(8,128)S(1)} %fusion, f32[512,768]{1,0:T(8,128)S(1)} %copy-done.9), kind=kOutput, calls=%fused_computation.4 | convolution fusion | flops 1616642048 | bytes 14155776 | tf_op jit(solution)/shard_map/dot_general | solution.py:24
  124.9 4.9 %all-to-all-start.3 = ((bf16[16,32,2048]{2,1,0:T(8,128)(2,1)}), bf16[16,32,2048]{2,1,0:T(8,128)(2,1)}, u32[]{:S(2)}, u32[]{:S(2)}) async-start(bf16[16,32,2048]{2,1,0:T(8,128)(2,1)} %bitcast.62), calls=%async_computation.3 | async-start | bytes 4194304 | tf_op jit(solution)/shard_map/all_to_all | solution.py:76
  129.8 6.0 %fusion.12 = bf16[512,2048]{1,0:T(8,128)(2,1)} fusion(bf16[1,768,2048]{2,1,0:T(8,128)(2,1)} %param.17, f32[512,768]{1,0:T(8,128)} %fusion.6, f32[512,768]{1,0:T(8,128)} %fusion.10), kind=kOutput, calls=%fused_computation.17 | convolution fusion | flops 1614020608 | bytes 8388608 | tf_op jit(solution)/shard_map/dot_general | solution.py:12
  135.8 41.6 %all-to-all-done.3 = bf16[16,32,2048]{2,1,0:T(8,128)(2,1)} async-done(((bf16[16,32,2048]{2,1,0:T(8,128)(2,1)}), bf16[16,32,2048]{2,1,0:T(8,128)(2,1)}, u32[]{:S(2)}, u32[]{:S(2)}) %all-to-all-start.3) | async-done | bytes 2097184 | tf_op jit(solution)/shard_map/all_to_all | solution.py:76
  177.4 5.0 %all-to-all-start.1 = ((bf16[16,32,2048]{2,1,0:T(8,128)(2,1)}), bf16[16,32,2048]{2,1,0:T(8,128)(2,1)}, u32[]{:S(2)}, u32[]{:S(2)}) async-start(bf16[16,32,2048]{2,1,0:T(8,128)(2,1)} %bitcast.61), calls=%async_computation.1 | async-start | bytes 4194304 | tf_op jit(solution)/shard_map/all_to_all | solution.py:65
  182.4 0.1 reshape.89
  182.5 0.1 copy.17
  182.6 5.2 %gather_fusion.1 = bf16[256,2048]{1,0:T(8,128)(2,1)} fusion(bf16[512,2048]{1,0:T(8,128)(2,1)} %bitcast.12, s32[1024]{0:T(1024)S(1)} %pad_clamp_fusion.1), kind=kCustom, calls=%fused_computation.3 | custom fusion | bytes 2098176 | tf_op jit(solution)/shard_map/gather | solution.py:84
  187.8 42.1 %all-to-all-done.1 = bf16[16,32,2048]{2,1,0:T(8,128)(2,1)} async-done(((bf16[16,32,2048]{2,1,0:T(8,128)(2,1)}), bf16[16,32,2048]{2,1,0:T(8,128)(2,1)}, u32[]{:S(2)}, u32[]{:S(2)}) %all-to-all-start.1) | async-done | bytes 2097184 | tf_op jit(solution)/shard_map/all_to_all | solution.py:65
  229.9 5.2 %gather_fusion = bf16[256,2048]{1,0:T(8,128)(2,1)} fusion(bf16[512,2048]{1,0:T(8,128)(2,1)} %bitcast.7, s32[1024]{0:T(1024)S(1)} %pad_clamp_fusion.1), kind=kCustom, calls=%fused_computation.2 | custom fusion | bytes 2098176 | tf_op jit(solution)/shard_map/gather | solution.py:83
  235.1 3.4 %fusion.17 = (f32[32,2048]{1,0:T(8,128)S(1)}, f32[32,2048]{1,0:T(8,128)S(1)}) fusion(bf16[256,2048]{1,0:T(8,128)(2,1)} %gather_fusion.1, f32[32,8]{1,0:T(8,128)S(1)} %copy.17, bf16[256,2048]{1,0:T(8,128)(2,1)} %gather_fusion), kind=kLoop, calls=%fused_computation.22 | loop fusion | flops 3014656 | bytes 2622464 | tf_op jit(solution)/shard_map/reduce_sum | solution.py:87
  238.5 0.0 copy-done.4
  238.5 0.0 copy-done.2
  238.5 0.8 subtract_divide_fusion
  239.3 1.9 gather_fusion.2
  241.3 3.3 %gather_fusion.3 = f32[128,2048]{1,0:T(8,128)} fusion(f32[32,2048]{1,0:T(8,128)} %subtract_divide_fusion, s32[1024]{0:T(1024)S(1)} %pad_clamp_fusion), kind=kCustom, calls=%fused_computation.1.clone | custom fusion | bytes 2097664 | tf_op jit(solution)/shard_map/jit(_take)/gather | solution.py:90
  244.6 3.6 %select_add_fusion = (f32[128,2048]{1,0:T(8,128)}, f32[128,2048]{1,0:T(8,128)}) fusion(f32[128,2048]{1,0:T(8,128)} %gather_fusion.3, bf16[128,2048]{1,0:T(8,128)(2,1)} %param.11, pred[128]{0:T(512)(128)(4,1)S(1)} %compare_and_fusion, f32[128,2048]{1,0:T(8,128)} %gather_fusion.2, bf16[128,2048]{1,0:T(8,128)(2,1)} %param.10), kind=kLoop, calls=%fused_computation.29 | loop fusion | flops 1572864 | bytes 5243008 | tf_op jit(solution)/shard_map/add | solution.py:90
  (17 shorter events, 0.1 us)
Async XLA Ops:
  0.6 71.8 %copy-start = (bf16[1,2048,768]{2,1,0:T(8,128)(2,1)S(1)}, bf16[1,2048,768]{2,1,0:T(8,128)(2,1)}, u32[]{:S(2)}) copy-start(bf16[1,2048,768]{2,1,0:T(8,128)(2,1)} %param.16) | copy-start | bytes 9437188
  5.0 0.7 copy-start.3
  7.8 6.7 %copy-start.6 = (s32[128]{0:T(128)S(1)}, s32[128]{0:T(128)}, u32[]{:S(2)}) copy-start(s32[128]{0:T(128)} %param.12) | copy-start | bytes 1540
  7.8 54.2 %all-to-all-start = ((bf16[16,32,2048]{2,1,0:T(8,128)(2,1)}), bf16[16,32,2048]{2,1,0:T(8,128)(2,1)}, u32[]{:S(2)}, u32[]{:S(2)}) async-start(bf16[16,32,2048]{2,1,0:T(8,128)(2,1)} %bitcast.60), calls=%async_computation | async-start | bytes 4194304 | tf_op jit(solution)/shard_map/all_to_all | solution.py:61
  15.8 0.7 copy-start.1
  62.0 52.4 %all-to-all-start.2 = ((bf16[16,32,2048]{2,1,0:T(8,128)(2,1)}), bf16[16,32,2048]{2,1,0:T(8,128)(2,1)}, u32[]{:S(2)}, u32[]{:S(2)}) async-start(bf16[16,32,2048]{2,1,0:T(8,128)(2,1)} %bitcast.59), calls=%async_computation.2 | async-start | bytes 4194304 | tf_op jit(solution)/shard_map/all_to_all | solution.py:72
  114.5 4.5 %copy-start.8 = (f32[512,768]{1,0:T(8,128)S(1)}, f32[512,768]{1,0:T(8,128)}, u32[]{:S(2)}) copy-start(f32[512,768]{1,0:T(8,128)} %fusion.10) | copy-start | bytes 4718596
  119.0 1.9 copy-start.7
  119.0 2.3 copy-start.9
  124.9 52.4 %all-to-all-start.3 = ((bf16[16,32,2048]{2,1,0:T(8,128)(2,1)}), bf16[16,32,2048]{2,1,0:T(8,128)(2,1)}, u32[]{:S(2)}, u32[]{:S(2)}) async-start(bf16[16,32,2048]{2,1,0:T(8,128)(2,1)} %bitcast.62), calls=%async_computation.3 | async-start | bytes 4194304 | tf_op jit(solution)/shard_map/all_to_all | solution.py:76
  177.4 5.1 %copy-start.5 = (f32[32,8]{0,1:T(8,128)S(1)}, f32[32,8]{0,1:T(8,128)}, u32[]{:S(2)}) copy-start(f32[32,8]{0,1:T(8,128)} %param.14) | copy-start | bytes 3076
  177.4 52.6 %all-to-all-start.1 = ((bf16[16,32,2048]{2,1,0:T(8,128)(2,1)}), bf16[16,32,2048]{2,1,0:T(8,128)(2,1)}, u32[]{:S(2)}, u32[]{:S(2)}) async-start(bf16[16,32,2048]{2,1,0:T(8,128)(2,1)} %bitcast.61), calls=%async_computation.1 | async-start | bytes 4194304 | tf_op jit(solution)/shard_map/all_to_all | solution.py:65
  235.1 3.4 %copy-start.4 = (f32[32,2048]{1,0:T(8,128)S(1)}, f32[32,2048]{1,0:T(8,128)}, u32[]{:S(2)}) copy-start(f32[32,2048]{1,0:T(8,128)} %copy-done.3) | copy-start | bytes 786436
  235.1 3.4 %copy-start.2 = (f32[32,2048]{1,0:T(8,128)S(1)}, f32[32,2048]{1,0:T(8,128)}, u32[]{:S(2)}) copy-start(f32[32,2048]{1,0:T(8,128)} %copy-done.1) | copy-start | bytes 786436
where the time goes:
time: 249 us; the launch traced here: 248 us
  waiting for transfers between devices  165 us (66%)
  matrix products  32.6 us (13%)
  starting transfers between devices  21.6 us (9%)
  local copies, waits for them, and re-layouts  19.1 us (8%)
  other arithmetic  9.52 us (4%)
    all_to_all x1, waiting for transfers between devices, per_device(): lax.all_to_all(send_cent, 'expert', split_axis=0, concat_axis=0, tiled=True)  43.5 us
    all_to_all x1, waiting for transfers between devices, per_device(): lax.all_to_all(output.reshape(experts, capacity, model_width), 'expert',...  42.1 us
    all_to_all x1, waiting for transfers between devices, per_device(): lax.all_to_all(input_grad.reshape(experts, capacity, model_width), 'exper...  41.6 us
    all_to_all x1, waiting for transfers between devices, per_device(): lax.all_to_all(send_grad, 'expert', split_axis=0, concat_axis=0, tiled=True)  37.5 us
    all_to_all x1, starting transfers between devices, per_device(): lax.all_to_all(send_cent, 'expert', split_axis=0, concat_axis=0, tiled=True)  6.69 us
    dot_general x1, matrix products, expert_forward(): jnp.dot(hidden, down_mat, preferred_element_type=jnp.float32)  5.97 us
    dot_general x1, matrix products, expert_forward(): gate_act = jnp.dot(inputs, gate_mat, preferred_element_type=jnp.float32)  5.45 us
    gather x1, local copies, waits for them, and re-layouts, per_device(): returned_grad = results_grad.reshape(-1, model_width)[slot_of]  5.19 us
  transfers between devices with their start and end apart: 4, of which 4 were waited for; matrix products, arithmetic and copies ran while one was open for 10% of the time, Pallas kernels for 0%

commit v1 on v0

--- a/solution.py
+++ b/solution.py
@@ -93,6 +93,55 @@
     return (layer_out, token_grad)
 
 
+def dense_per_device(
+    tokens, out_grad, cluster_ids, routes, route_weights, gate_weight, up_weight, down_weight
+):
+    cent_rows = routes.shape[0]
+    experts = lax.axis_size("expert")
+    me = lax.axis_index("expert")
+    member = (cluster_ids[:, None] == jnp.arange(cent_rows, dtype=jnp.int32)[None, :]).astype(
+        jnp.bfloat16
+    )
+    counts = jnp.sum(member.astype(jnp.float32), axis=0)
+    contract = (((0,), (0,)), ((), ()))
+    centroid = (
+        lax.dot_general(member, tokens, contract, preferred_element_type=jnp.float32)
+        / counts[:, None]
+    )
+    grad_sum = lax.dot_general(member, out_grad, contract, preferred_element_type=jnp.float32)
+    spread = jnp.sum(
+        jnp.where(
+            routes[:, :, None] == jnp.arange(experts, dtype=jnp.int32)[None, None, :],
+            route_weights[:, :, None],
+            0.0,
+        ),
+        axis=1,
+    )
+    share = lax.all_gather(spread, "expert", axis=0, tiled=True)
+    mine = lax.dynamic_slice_in_dim(share, me, 1, axis=1)
+    arrived = lax.all_gather(centroid.astype(jnp.bfloat16), "expert", axis=0, tiled=True)
+    arrived_grad = lax.all_gather(grad_sum.astype(jnp.bfloat16), "expert", axis=0, tiled=True)
+    gate_mat = gate_weight[0]
+    up_mat = up_weight[0]
+    down_mat = down_weight[0]
+    output, gate_act, up_act = expert_forward(arrived, gate_mat, up_mat, down_mat)
+    combined = lax.psum_scatter(
+        output.astype(jnp.float32) * mine, "expert", scatter_dimension=0, tiled=True
+    )
+    input_grad = expert_backward(arrived_grad, gate_act, up_act, gate_mat, up_mat, down_mat)
+    centroid_grad = (
+        lax.psum_scatter(
+            input_grad.astype(jnp.float32) * mine, "expert", scatter_dimension=0, tiled=True
+        )
+        - grad_sum
+    )
+    layer_out = tokens.astype(jnp.float32) + jnp.take(combined - centroid, cluster_ids, axis=0)
+    token_grad = out_grad.astype(jnp.float32) + jnp.take(
+        centroid_grad / counts[:, None], cluster_ids, axis=0
+    )
+    return (layer_out, token_grad)
+
+
 def solution(mesh):
     placed = (
         P(("groups", "expert"), None),
@@ -104,8 +153,9 @@
         P("expert", None, None),
         P("expert", None, None),
     )
+    dense = mesh.shape["expert"] <= 16
     return jax.shard_map(
-        per_device,
+        dense_per_device if dense else per_device,
         mesh=mesh,
         in_specs=placed,
         out_specs=(P(("groups", "expert"), None), P(("groups", "expert"), None)),

time: 249 us -> 261 us (1.048)
  the two profiles are of different devices: /device:TPU:13 before, /device:TPU:0 now
where the time goes in v1:
time: 261 us
  waiting for transfers between devices  186 us (71%)
  matrix products  23.8 us (9%)
  blocking collectives  23.5 us (9%)
  between operations  13.9 us (5%)
  other arithmetic  6.71 us (3%)
  local copies, waits for them, and re-layouts  6.34 us (2%)
    reduce_scatter x1, waiting for transfers between devices, dense_per_device(): lax.psum_scatter(input_grad.astype(jnp.float32) * mine, 'expert', scatter...  72.8 us
    reduce_scatter x1, waiting for transfers between devices, dense_per_device(): lax.psum_scatter(output.astype(jnp.float32) * mine, 'expert', scatter_dim...  64.1 us
    all_gather x1, waiting for transfers between devices, dense_per_device(): lax.all_gather(grad_sum.astype(jnp.bfloat16), 'expert', axis=0, tiled=True)  30.9 us
    all_gather x1, blocking collectives, dense_per_device(): share = lax.all_gather(spread, 'expert', axis=0, tiled=True)  23.5 us
    all_gather x1, waiting for transfers between devices, dense_per_device(): lax.all_gather(centroid.astype(jnp.bfloat16), 'expert', axis=0, tiled=True)  18.5 us
  transfers between devices with their start and end apart: 4, of which 4 were waited for; matrix products, arithmetic and copies ran while one was open for 10% of the time, Pallas kernels for 0%

profile of v1, /device:TPU:0, one launch (start us, length us, event | category | flops | bytes accessed | tf_op | source)
XLA Modules:
  0.0 260.9 jit_solution(8647642838947983499)
XLA Ops:
  7.2 0.0 copy-start
  7.2 0.0 copy-start.1
  7.2 0.0 copy-start.2
  7.2 0.0 all-gather.4.cloned.1.call-start
  7.2 0.9 convert_reduce_fusion
  8.2 2.0 fusion.32
  10.2 0.0 all-gather.4.cloned.1.call-update
  10.2 0.0 all-gather.6.cloned.1.call-start
  10.2 2.0 fusion.31
  12.2 0.0 all-gather.6.cloned.1.call-update
  12.3 0.0 reduce-scatter.3.cloned.1.call-start
  12.3 0.0 copy-done.1
  12.3 0.0 copy-done.2
  12.3 23.5 %all-gather = f32[16,32,16]{1,2,0:T(8,128)S(1)} all-gather(f32[1,32,16]{1,2,0:T(8,128)S(1)} %bitcast.32), channel_id=1, replica_groups=mesh['groups'=2,'expert'=16] {'expert'}, dimensions={0}, use_global_device_ids=true | all-gather | bytes 34816 | tf_op jit(solution)/shard_map/all_gather | solution.py:120
  35.9 0.1 reshape.32
  36.0 18.5 %all-gather.4.cloned.1.call-done = bf16[512,2048]{1,0:T(8,128)(2,1)} async-done(((bf16[32,2048]{1,0:T(8,128)(2,1)}), bf16[512,2048]{1,0:T(8,128)(2,1)}) %all-gather.4.cloned.1.call-update) | async-done | bytes 2097168 | tf_op jit(solution)/shard_map/all_gather | solution.py:122
  54.5 0.0 copy-start.4
  54.6 4.5 %fusion.10 = f32[512,768]{1,0:T(8,128)S(1)} fusion(bf16[512,2048]{1,0:T(8,128)(2,1)} %all-gather.4.cloned.1.call-done, bf16[1,2048,768]{2,1,0:T(8,128)(2,1)} %param.15), kind=kOutput, calls=%fused_computation.15 | convolution fusion | flops 1610612736 | bytes 6815744 | tf_op jit(solution)/shard_map/dot_general | solution.py:8
  59.0 0.0 copy-done.4
  59.0 0.0 copy-done.7
  59.0 0.0 copy-start.8
  59.0 1.8 fusion.6
  60.9 0.0 copy-start.10
  60.9 0.0 copy-done.8
  60.9 1.2 copy-done.10
  62.1 0.0 copy-done
  62.1 3.8 %convert_multiply_fusion.1 = f32[512,2048]{1,0:T(8,128)} fusion(bf16[1,768,2048]{2,1,0:T(8,128)(2,1)S(1)} %copy-done, f32[512]{0:T(512)S(1)} %bitcast.33, f32[512,768]{1,0:T(8,128)S(1)} %fusion.6, f32[512,768]{1,0:T(8,128)S(1)} %fusion.10), kind=kOutput, calls=%fused_computation.4 | convolution fusion | flops 1616117760 | bytes 10487808 | tf_op jit(solution)/shard_map/dot_general | solution.py:12
  65.9 0.0 reduce-scatter.3.cloned.1.call-update
  65.9 0.0 reduce-scatter.5.cloned.1.call-start
  66.0 30.9 %all-gather.6.cloned.1.call-done = bf16[512,2048]{1,0:T(8,128)(2,1)} async-done(((bf16[32,2048]{1,0:T(8,128)(2,1)}), bf16[512,2048]{1,0:T(8,128)(2,1)}) %all-gather.6.cloned.1.call-update) | async-done | bytes 2097168 | tf_op jit(solution)/shard_map/all_gather | solution.py:123
  96.9 3.6 %fusion = f32[512,768]{1,0:T(8,128)S(1)} fusion(bf16[512,2048]{1,0:T(8,128)(2,1)} %all-gather.6.cloned.1.call-done, bf16[1,768,2048]{2,1,0:T(8,128)(2,1)S(1)} %copy-done), kind=kOutput, calls=%fused_computation.5 | convolution fusion | flops 1610612736 | bytes 6815744 | tf_op jit(solution)/shard_map/dot_general | solution.py:18
  100.5 0.0 copy-done.5
  100.5 0.0 copy-done.9
  100.5 0.0 copy-start.6
  100.5 0.0 copy-start.11
  100.5 1.9 fusion.4
  102.4 0.0 copy-done.6
  102.4 0.4 copy-done.11
  102.9 4.3 %convert_multiply_fusion = f32[512,2048]{1,0:T(8,128)} fusion(f32[512,2048]{1,0:T(8,128)S(1)} %fusion.4, bf16[1,2048,768]{2,1,0:T(8,128)(2,1)S(1)} %copy-done.6, f32[512]{0:T(512)S(1)} %bitcast.34, f32[512,768]{1,0:T(8,128)S(1)} %copy-done.9, f32[512,768]{1,0:T(8,128)S(1)} %fusion, f32[512,768]{1,0:T(8,128)S(1)} %copy-done.11), kind=kOutput, calls=%fused_computation.2 | convolution fusion | flops 1618739200 | bytes 16254976 | tf_op jit(solution)/shard_map/dot_general | solution.py:24
  107.1 0.0 reduce-scatter.5.cloned.1.call-update
  107.2 0.6 copy-done.3
  107.8 64.1 %reduce-scatter.3.cloned.1.call-done = f32[32,2048]{1,0:T(8,128)} async-done(((f32[512,2048]{1,0:T(8,128)}), f32[32,2048]{1,0:T(8,128)}) %reduce-scatter.3.cloned.1.call-update) | async-done | bytes 262160 | tf_op jit(solution)/shard_map/reduce_scatter | solution.py:128
  171.9 1.1 sub.9
  173.0 1.9 gather_fusion
  174.9 72.8 %reduce-scatter.5.cloned.1.call-done = f32[32,2048]{1,0:T(8,128)} async-done(((f32[512,2048]{1,0:T(8,128)}), f32[32,2048]{1,0:T(8,128)}) %reduce-scatter.5.cloned.1.call-update) | async-done | bytes 262160 | tf_op jit(solution)/shard_map/reduce_scatter | solution.py:133
  247.7 1.1 subtract_divide_fusion
  248.9 1.9 gather_fusion.1
  250.8 3.6 %select_add_fusion = (f32[128,2048]{1,0:T(8,128)}, f32[128,2048]{1,0:T(8,128)}) fusion(f32[128,2048]{1,0:T(8,128)} %gather_fusion.1, bf16[128,2048]{1,0:T(8,128)(2,1)} %param.11, pred[128]{0:T(512)(128)(4,1)S(1)} %compare_and_fusion, f32[128,2048]{1,0:T(8,128)} %gather_fusion, bf16[128,2048]{1,0:T(8,128)(2,1)} %param.10), kind=kLoop, calls=%fused_computation.23 | loop fusion | flops 1572864 | bytes 5243008 | tf_op jit(solution)/shard_map/add | solution.py:139
  (10 shorter events, 0.1 us)
Async XLA Ops:
  7.2 54.9 %copy-start = (bf16[1,768,2048]{2,1,0:T(8,128)(2,1)S(1)}, bf16[1,768,2048]{2,1,0:T(8,128)(2,1)}, u32[]{:S(2)}) copy-start(bf16[1,768,2048]{2,1,0:T(8,128)(2,1)} %param.17) | copy-start | bytes 9437188
  7.2 5.1 %copy-start.1 = (f32[32,8]{0,1:T(8,128)S(1)}, f32[32,8]{0,1:T(8,128)}, u32[]{:S(2)}) copy-start(f32[32,8]{0,1:T(8,128)} %param.14) | copy-start | bytes 3076
  7.2 5.1 %copy-start.2 = (s32[32,8]{0,1:T(8,128)S(1)}, s32[32,8]{0,1:T(8,128)}, u32[]{:S(2)}) copy-start(s32[32,8]{0,1:T(8,128)} %param.13) | copy-start | bytes 3076
  7.2 47.3 %all-gather.4.cloned.1.call-start = ((), (), s32[]{:S(2)}) async-start(), calls=%async_computation.2 | async-start | bytes 2228224 | tf_op jit(solution)/shard_map/all_gather | solution.py:122
  10.2 86.7 %all-gather.6.cloned.1.call-start = ((), (), s32[]{:S(2)}) async-start(), calls=%async_computation.4 | async-start | bytes 2228224 | tf_op jit(solution)/shard_map/all_gather | solution.py:123
  12.3 159.7 %reduce-scatter.3.cloned.1.call-start = ((), (), s32[]{:S(2)}) async-start(), calls=%async_computation.3 | async-start | bytes 4456448 | tf_op jit(solution)/shard_map/reduce_scatter | solution.py:128
  54.5 4.5 %copy-start.4 = (bf16[1,2048,768]{2,1,0:T(8,128)(2,1)S(1)}, bf16[1,2048,768]{2,1,0:T(8,128)(2,1)}, u32[]{:S(2)}) copy-start(bf16[1,2048,768]{2,1,0:T(8,128)(2,1)} %param.16) | copy-start | bytes 9437188
  54.5 4.5 %copy-start.7 = (bf16[512,2048]{1,0:T(8,128)(2,1)S(1)}, bf16[512,2048]{1,0:T(8,128)(2,1)}, u32[]{:S(2)}) copy-start(bf16[512,2048]{1,0:T(8,128)(2,1)} %all-gather.4.cloned.1.call-done) | copy-start | bytes 6291460
  59.0 1.8 copy-start.8
  60.9 1.2 copy-start.10
  65.9 181.8 %reduce-scatter.5.cloned.1.call-start = ((), (), s32[]{:S(2)}) async-start(), calls=%async_computation.5 | async-start | bytes 4456448 | tf_op jit(solution)/shard_map/reduce_scatter | solution.py:133
  96.9 3.6 %copy-start.5 = (bf16[1,2048,768]{2,1,0:T(8,128)(2,1)S(1)}, bf16[1,2048,768]{2,1,0:T(8,128)(2,1)}, u32[]{:S(2)}) copy-start(bf16[1,2048,768]{2,1,0:T(8,128)(2,1)} %param.16) | copy-start | bytes 9437188
  96.9 3.6 %copy-start.9 = (f32[512,768]{1,0:T(8,128)S(1)}, f32[512,768]{1,0:T(8,128)}, u32[]{:S(2)}) copy-start(f32[512,768]{1,0:T(8,128)} %copy-done.8) | copy-start | bytes 4718596
  100.5 1.9 copy-start.6
  100.5 2.3 copy-start.11
  107.1 0.7 copy-start.3
Sparse Core Ops, SparseCore 0:
  10.3 44.1 all-gather.3
  56.7 40.1 all-gather.5
  100.8 71.1 reduce-scatter.2
  176.1 71.5 reduce-scatter.4
